TPU v7x, 32 devices: a whole 2x2x4 slice. The times are simulated.
32 devices in a mesh: rows: 16 (over z, y, x), seq: 2 (over core).
Axes of the slice: x: 2, y: 2, z: 4, core: 2. Of those that a mesh axis runs over, the one named last changes fastest.
Arguments:
- tokens_a: bfloat16 [64, 512, 768], P('rows', 'seq'), may hold values from -6 to 6
- lengths_a: int32 [64], P('rows'), may hold values from 128 to 512, as said below
- cotangent_a: bfloat16 [64, 512, 768], P('rows', 'seq'), may hold values from -6 to 6
- tokens_b: bfloat16 [128, 256, 768], P('rows', 'seq'), may hold values from -6 to 6
- lengths_b: int32 [128], P('rows'), may hold values from 64 to 256, as said below
- cotangent_b: bfloat16 [128, 256, 768], P('rows', 'seq'), may hold values from -6 to 6
- gain_attn: float32 [768], replicated, may hold values from 0.25 to 1.75
- w_query: bfloat16 [768, 768], replicated, may hold values from -0.0546875 to 0.0546875
- w_key: bfloat16 [768, 768], replicated, may hold values from -0.21875 to 0.21875
- w_value: bfloat16 [768, 768], replicated, may hold values from -0.21875 to 0.21875
- w_out: bfloat16 [768, 768], replicated, may hold values from -0.875 to 0.875
- relative_bias_table: float32 [32, 12], replicated, may hold values from -4 to 4
- gain_ffn: float32 [768], replicated, may hold values from 0.25 to 1.75
- w_in: bfloat16 [768, 3072], replicated, may hold values from -0.21875 to 0.21875
- w_back: bfloat16 [3072, 768], replicated, may hold values from -0.15625 to 0.15625
Outputs:
- out_a: bfloat16 [64, 512, 768], P('rows', 'seq')
- out_b: bfloat16 [128, 256, 768], P('rows', 'seq')
- grad_tokens_a: bfloat16 [64, 512, 768], P('rows', 'seq')
- grad_tokens_b: bfloat16 [128, 256, 768], P('rows', 'seq')
- grad_gain_attn: float32 [768], replicated
- grad_query: float32 [768, 768], P('rows', 'seq')
- grad_key: float32 [768, 768], P('rows', 'seq')
- grad_value: float32 [768, 768], P('rows', 'seq')
- grad_out: float32 [768, 768], P('rows', 'seq')
- grad_table: float32 [32, 12], replicated
- grad_gain_ffn: float32 [768], replicated
- grad_in: float32 [768, 3072], P('rows', 'seq')
- grad_back: float32 [3072, 768], P('rows', 'seq')
Inputs may be any that keep to these rules, and one draw needn't show every extreme that they name: `lengths_a`: real tokens of each sequence; keys at positions at or beyond it are padding. In every draw some sequence has exactly 512. `lengths_b`: real tokens of each sequence; keys at positions at or beyond it are padding. In every draw some sequence has exactly 256.
All inputs are finite; a program needn't handle non-finite values.
Results may differ from a plain program's by a relative error of at most 0.015.
Values may be sent and summed in bfloat16 or wider, within the bound.
No kernel may reach another device: no remote copies, remote signals or barrier semaphores. Data moves between devices by JAX's collectives and lax.ppermute only.
A program may use at most 384 MiB of HBM per device.

v0:
```python
import jax
import jax.numpy as jnp
from jax import lax
from jax.sharding import PartitionSpec as P

epsilon = 1e-06
topmost_precision = lax.Precision.HIGHEST
bucket_edges = (12, 16, 23, 32, 46, 64, 91)
masked_score = -1e30
gelu_coef = 0.7978845608
cubic_coef = 0.044715


def for_sending(value):

    def short(part):
        return part.astype(jnp.bfloat16) if part.dtype == jnp.float32 else part

    return jax.tree.map(short, value)


def gelu_tanh(value_in):
    return (
        0.5
        * value_in
        * (1.0 + jnp.tanh(gelu_coef * (value_in + cubic_coef * value_in * value_in * value_in)))
    )


def gelu_slope(value_in):
    bent = jnp.tanh(gelu_coef * (value_in + cubic_coef * value_in * value_in * value_in))
    return 0.5 * (1.0 + bent) + 0.5 * value_in * (1.0 - bent * bent) * gelu_coef * (
        1.0 + 3.0 * cubic_coef * value_in * value_in
    )


def bucket_ids(query_pos, key_pos, buckets):
    offset = key_pos[None, :] - query_pos[:, None]
    distance = jnp.abs(offset)
    far_part = 8 + sum(((distance >= edge_value).astype(jnp.int32) for edge_value in bucket_edges))
    return jnp.where(distance < 8, distance, far_part) + buckets // 2 * (offset > 0).astype(
        jnp.int32
    )


def inv_rms(array_in):
    return lax.rsqrt(jnp.mean(array_in * array_in, axis=-1, keepdims=True) + epsilon)


def project(left_operand, weight_matrix):
    return jnp.einsum(
        "ung,gr->unr", left_operand, weight_matrix, preferred_element_type=jnp.float32
    )


def back_project(gradient_half, weight_matrix):
    return jnp.einsum(
        "kyz,vz->kyv", gradient_half, weight_matrix, preferred_element_type=jnp.float32
    )


def weight_grad(left_operand, right_operand):
    return jnp.einsum(
        "hyk,hyg->kg", left_operand, right_operand, preferred_element_type=jnp.float32
    )


def add_pair(first_term, second_term):
    return first_term + second_term


def layer_bucket(tokens, lengths, cotangent, params):
    gain_attn, w_query, w_key, w_value, w_out, relative_bias_table, gain_ffn, w_in, w_back = params
    seqs_here, local_len, feature_width = tokens.shape
    buckets, head_count = relative_bias_table.shape
    head_size = feature_width // head_count
    full_len = local_len * lax.axis_size("seq")
    query_pos = lax.axis_index("seq") * local_len + jnp.arange(local_len, dtype=jnp.int32)
    key_pos = jnp.arange(full_len, dtype=jnp.int32)
    bucket_range = jnp.arange(buckets, dtype=jnp.int32)[:, None, None]
    bucket_indicator = (bucket_ids(query_pos, key_pos, buckets)[None] == bucket_range).astype(
        jnp.float32
    )
    relative_position_bias = jnp.einsum(
        "mfi,mz->zfi", bucket_indicator, relative_bias_table, precision=topmost_precision
    )
    key_live = key_pos[None, None, None, :] < lengths[:, None, None, None]

    def to_heads(array_in, length_now):
        return array_in.reshape(seqs_here, length_now, head_count, head_size)

    tokens_f = tokens.astype(jnp.float32)
    scale_one = inv_rms(tokens_f)
    normed = (tokens_f * scale_one * gain_attn).astype(jnp.bfloat16)
    query_low = project(normed, w_query).astype(jnp.bfloat16)
    keys_local = project(normed, w_key).astype(jnp.bfloat16)
    values_local = project(normed, w_value).astype(jnp.bfloat16)
    keys_all, values_all = (
        lax.all_gather(keys_local, "seq", axis=1, tiled=True),
        lax.all_gather(values_local, "seq", axis=1, tiled=True),
    )
    query_heads = to_heads(query_low, local_len)
    raw_scores = jnp.einsum(
        "sqhe,skhe->shqk",
        query_heads,
        to_heads(keys_all, full_len),
        preferred_element_type=jnp.float32,
    )
    scores = jnp.where(key_live, raw_scores + relative_position_bias[None], masked_score)
    row_max = jnp.max(scores, axis=-1, keepdims=True)
    exp_scores = jnp.exp(scores - row_max)
    row_total = jnp.sum(exp_scores, axis=-1, keepdims=True)
    attn_probs = exp_scores / row_total
    probs_low = attn_probs.astype(jnp.bfloat16)
    attn_mixed = jnp.einsum(
        "shqk,skhe->sqhe",
        probs_low,
        to_heads(values_all, full_len),
        preferred_element_type=jnp.float32,
    )
    attn_mixed = attn_mixed.reshape(seqs_here, local_len, feature_width).astype(jnp.bfloat16)
    hidden = tokens_f + project(attn_mixed, w_out)
    scale_two = inv_rms(hidden)
    normed_two = (hidden * scale_two * gain_ffn).astype(jnp.bfloat16)
    inner_pre = project(normed_two, w_in)
    inner_low = gelu_tanh(inner_pre).astype(jnp.bfloat16)
    output = (hidden + project(inner_low, w_back)).astype(jnp.bfloat16)
    grad_back = weight_grad(inner_low, cotangent)
    d_inner = (back_project(cotangent, w_back) * gelu_slope(inner_pre)).astype(jnp.bfloat16)
    grad_in = weight_grad(normed_two, d_inner)
    d_normed_two = back_project(d_inner, w_in)
    gained_two = d_normed_two * gain_ffn
    d_hidden = (
        cotangent.astype(jnp.float32)
        + scale_two * gained_two
        - hidden * scale_two**3 * jnp.mean(gained_two * hidden, axis=-1, keepdims=True)
    )
    gain_two_grad = jnp.sum(d_normed_two * hidden * scale_two, axis=(0, 1))
    d_hidden_low = d_hidden.astype(jnp.bfloat16)
    grad_out = weight_grad(attn_mixed, d_hidden_low)
    d_attn = back_project(d_hidden_low, w_out).astype(jnp.bfloat16)
    d_attn_heads = to_heads(d_attn, local_len)
    keys_back, values_back = (keys_all, values_all)
    d_probs = jnp.einsum(
        "sqhe,skhe->shqk",
        d_attn_heads,
        to_heads(values_back, full_len),
        preferred_element_type=jnp.float32,
    )
    row_delta = jnp.sum(attn_probs * d_probs, axis=-1, keepdims=True)
    score_gradient = attn_probs * (d_probs - row_delta)
    d_scores_low = score_gradient.astype(jnp.bfloat16)
    d_query = jnp.einsum(
        "shqk,skhe->sqhe",
        d_scores_low,
        to_heads(keys_back, full_len),
        preferred_element_type=jnp.float32,
    )
    d_query = d_query.reshape(seqs_here, local_len, feature_width).astype(jnp.bfloat16)
    bias_table_gradient = jnp.einsum(
        "rgtj,etj->eg", score_gradient, bucket_indicator, precision=topmost_precision
    )
    key_part = jnp.einsum(
        "shqk,sqhe->skhe", d_scores_low, query_heads, preferred_element_type=jnp.float32
    ).reshape(seqs_here, full_len, feature_width)
    value_part = jnp.einsum(
        "shqk,sqhe->skhe", probs_low, d_attn_heads, preferred_element_type=jnp.float32
    ).reshape(seqs_here, full_len, feature_width)
    d_keys, d_values = (
        lax.psum_scatter(
            key_part.astype(jnp.bfloat16), "seq", scatter_dimension=1, tiled=True
        ).astype(jnp.float32),
        lax.psum_scatter(
            value_part.astype(jnp.bfloat16), "seq", scatter_dimension=1, tiled=True
        ).astype(jnp.float32),
    )
    d_keys = d_keys.astype(jnp.bfloat16)
    d_values = d_values.astype(jnp.bfloat16)
    grad_query = weight_grad(normed, d_query)
    grad_key = weight_grad(normed, d_keys)
    grad_value = weight_grad(normed, d_values)
    d_normed = (
        back_project(d_query, w_query)
        + back_project(d_keys, w_key)
        + back_project(d_values, w_value)
    )
    gained_one = d_normed * gain_attn
    d_tokens = (
        d_hidden
        + scale_one * gained_one
        - tokens_f * scale_one**3 * jnp.mean(gained_one * tokens_f, axis=-1, keepdims=True)
    )
    gain_one_grad = jnp.sum(d_normed * tokens_f * scale_one, axis=(0, 1))
    small_part = (gain_one_grad, bias_table_gradient, gain_two_grad)
    large_part = (grad_query, grad_key, grad_value, grad_out, grad_in, grad_back)
    return (output, d_tokens.astype(jnp.bfloat16), small_part, large_part)


def reduce_large(large_part):
    partial_sum = lax.psum_scatter(large_part, "rows", scatter_dimension=0, tiled=True)
    return jax.tree.map(
        lambda part: part.astype(jnp.float32),
        lax.psum_scatter(for_sending(partial_sum), "seq", scatter_dimension=1, tiled=True),
    )


def body(
    tokens_a,
    lengths_a,
    cotangent_a,
    tokens_b,
    lengths_b,
    cotangent_b,
    gain_attn,
    w_query,
    w_key,
    w_value,
    w_out,
    relative_bias_table,
    gain_ffn,
    w_in,
    w_back,
):
    params = (
        gain_attn,
        w_query,
        w_key,
        w_value,
        w_out,
        relative_bias_table,
        gain_ffn,
        w_in,
        w_back,
    )
    out_a, grad_a, small_a, large_a = layer_bucket(tokens_a, lengths_a, cotangent_a, params)
    out_b, grad_b, small_b, large_b = layer_bucket(tokens_b, lengths_b, cotangent_b, params)
    large_sum = reduce_large(jax.tree.map(add_pair, large_a, large_b))
    small_local = jax.tree.map(add_pair, small_a, small_b)
    gain_one, table_sum, gain_two = lax.psum(
        (small_local[0], small_local[1], small_local[2]), ("rows", "seq")
    )
    return (
        out_a,
        out_b,
        grad_a,
        grad_b,
        gain_one,
        large_sum[0],
        large_sum[1],
        large_sum[2],
        large_sum[3],
        table_sum,
        gain_two,
        large_sum[4],
        large_sum[5],
    )


def solution(mesh):
    placed = (
        P("rows", "seq", None),
        P("rows"),
        P("rows", "seq", None),
        P("rows", "seq", None),
        P("rows"),
        P("rows", "seq", None),
        P(),
        P(),
        P(),
        P(),
        P(),
        P(),
        P(),
        P(),
        P(),
    )
    return jax.shard_map(
        body,
        mesh=mesh,
        in_specs=placed,
        out_specs=(
            P("rows", "seq", None),
            P("rows", "seq", None),
            P("rows", "seq", None),
            P("rows", "seq", None),
            P(),
            P("rows", "seq"),
            P("rows", "seq"),
            P("rows", "seq"),
            P("rows", "seq"),
            P(),
            P(),
            P("rows", "seq"),
            P("rows", "seq"),
        ),
        check_vma=False,
    )
```

profile of v0, /device:TPU:0, one launch (start us, length us, event | category | flops | bytes accessed | tf_op | source)
XLA Modules:
  0.0 1429.0 jit_solution(7156115138278579330)
XLA Ops:
  51.7 185.7 %copy.103 = pred[32,256,512]{2,0,1:T(32,128)(4,1)S(1)} copy(pred[32,256,512]{1,0,2:T(32,128)(4,1)S(1)} %iota_compare_fusion) | data formatting | bytes 8388608 | tf_op jit(solution)/shard_map/eq | solution.py:81
  253.3 16.3 %fusion.155 = (f32[4,12,256]{2,1,0:T(8,128)S(1)}, f32[4,12,256,512]{3,2,1,0:T(8,128)}) fusion(f32[12,256,512]{2,1,0:T(8,128)} %copy.104, pred[4,512]{1,0:T(4,128)(4,1)S(1)} %iota_compare_fusion.3, bf16[4,256,12,64]{1,3,2,0:T(8,128)(2,1)} %bitcast.206, bf16[4,512,12,64]{1,3,2,0:T(8,128)(2,1)} %bitcast.203), kind=kOutput, calls=%fused_computation.215 | convolution fusion | flops 830472704 | bytes 36227072 | tf_op jit(solution)/shard_map/sub | solution.py:111
  274.2 12.8 fusion.83
  292.2 10.4 fusion.44
  302.7 14.8 %fusion.11 = bf16[4,256,3072]{2,1,0:T(8,128)(2,1)} fusion(f32[4,256,3072]{2,1,0:T(8,128)} %fusion.44, bf16[4,256,768]{2,1,0:T(8,128)(2,1)S(1)} %copy-done.22, bf16[3072,768]{1,0:T(8,128)(2,1)S(1)} %bitcast.242), kind=kOutput, calls=%fused_computation.20 | convolution fusion | flops 4891607040 | bytes 25165824 | tf_op jit(solution)/shard_map/kyz,vz->kyv/dot_general | solution.py:57
  322.1 10.2 multiply_reduce_fusion.3
  339.2 11.7 fusion.156
  364.2 11.8 fusion.42
  376.1 14.2 fusion.16
  390.3 10.7 multiply_reduce_fusion.2
  417.6 21.2 %multiply_reduce_fusion = (f32[4,12,256]{2,1,0:T(8,128)S(1)}, f32[4,12,256,512]{3,2,1,0:T(8,128)}) fusion(f32[4,12,256,512]{3,2,1,0:T(8,128)} %get-tuple-element.37, f32[4,12,256]{2,1,0:T(8,128)S(1)} %get-tuple-element.36, bf16[4,256,12,64]{1,3,2,0:T(8,128)(2,1)} %bitcast.227, bf16[4,512,12,64]{1,3,2,0:T(8,128)(2,1)} %bitcast.220), kind=kOutput, calls=%fused_computation.3 | convolution fusion | flops 824168448 | bytes 55148544 | tf_op jit(solution)/shard_map/sqhe,skhe->shqk/dot_general | solution.py:144
  438.8 25.1 %fusion.21 = (f32[12,256,512]{2,1,0:T(8,128)}, bf16[4,12,256,512]{3,2,1,0:T(8,128)(2,1)}) fusion(f32[4,12,256,512]{3,2,1,0:T(8,128)} %get-tuple-element.46, f32[4,12,256]{2,1,0:T(8,128)S(1)} %get-tuple-element.45, f32[4,12,256,512]{3,2,1,0:T(8,128)} %get-tuple-element.37, f32[4,12,256]{2,1,0:T(8,128)S(1)} %get-tuple-element.36), kind=kLoop, calls=%fused_computation.37 | loop fusion | flops 29884416 | bytes 69304320 | tf_op jit(solution)/shard_map/rgtj,etj->eg/reduce_sum | solution.py:160
  463.8 9.7 convolution_convert_fusion.2
  478.5 13.0 multiply_reduce_fusion.1
  491.6 10.4 fusion.30
  509.3 11.9 fusion.73
  564.8 114.1 %reduce-scatter.35.cloned.1.call-done = f32[48,768]{1,0:T(8,128)} async-done(((f32[768,768]{1,0:T(8,128)}), f32[48,768]{1,0:T(8,128)}) %reduce-scatter.35.cloned.1.call-update) | async-done | bytes 147472 | tf_op jit(solution)/shard_map/reduce_scatter | solution.py:200
  680.9 10.3 reduce-scatter.29.cloned.1.call-done
  739.7 10.3 fusion.154
  750.1 12.9 bitcast_add_fusion
  772.2 10.5 bitcast_add_fusion.1
  786.2 9.7 copy.128
  795.9 11.1 convolution_bitcast_fusion.3
  815.7 11.7 add_convert_fusion.1
  846.7 44.8 %reduce-scatter.39.cloned.1.call-done = f32[48,768]{1,0:T(8,128)} async-done(((f32[768,768]{1,0:T(8,128)}), f32[48,768]{1,0:T(8,128)}) %reduce-scatter.39.cloned.1.call-update) | async-done | bytes 147472 | tf_op jit(solution)/shard_map/reduce_scatter | solution.py:200
  898.1 126.5 %reduce-scatter.37.cloned.1.call-done = f32[48,768]{1,0:T(8,128)} async-done(((f32[768,768]{1,0:T(8,128)}), f32[48,768]{1,0:T(8,128)}) %reduce-scatter.37.cloned.1.call-update) | async-done | bytes 147472 | tf_op jit(solution)/shard_map/reduce_scatter | solution.py:200
  1033.4 41.6 %all-reduce = (f32[768]{0:T(1024)}, f32[32,12]{0,1:T(8,128)}, f32[768]{0:T(1024)}) all-reduce(f32[768]{0:T(1024)S(1)} %add.369, f32[32,12]{0,1:T(8,128)S(1)} %fusion.106, f32[768]{0:T(1024)S(1)} %add.375), channel_id=1, replica_groups=mesh['rows'=16,'seq'=2] {'rows','seq'}, use_global_device_ids=true, to_apply=%region_20.21 | all-reduce | flops 1920 | bytes 15360 | tf_op jit(solution)/shard_map/psum | solution.py:239
  1075.0 126.0 %reduce-scatter.47.cloned.1.call-done = f32[192,768]{1,0:T(8,128)} async-done(((f32[3072,768]{1,0:T(8,128)}), f32[192,768]{1,0:T(8,128)}) %reduce-scatter.47.cloned.1.call-update) | async-done | bytes 589840 | tf_op jit(solution)/shard_map/reduce_scatter | solution.py:200
  1207.3 170.2 %reduce-scatter.43.cloned.1.call-done = f32[48,3072]{1,0:T(8,128)} async-done(((f32[768,3072]{1,0:T(8,128)}), f32[48,3072]{1,0:T(8,128)}) %reduce-scatter.43.cloned.1.call-update) | async-done | bytes 589840 | tf_op jit(solution)/shard_map/reduce_scatter | solution.py:200
  1387.7 9.8 reduce-scatter.51.cloned.1.call-done
  1399.1 9.6 reduce-scatter.57.cloned.1.call-done
  1410.5 9.8 reduce-scatter.45.cloned.1.call-done
  (283 shorter events, 294.8 us)
Async XLA Ops:
  7.2 241.4 %all-gather.7.cloned.1.call-start = ((), (), s32[]{:S(2)}) async-start(), calls=%async_computation.17 | async-start | bytes 4718592 | tf_op jit(solution)/shard_map/all_gather | solution.py:99
  9.7 16.5 %copy-start.41 = (f32[4,256]{1,0:T(4,128)}, f32[4,256]{1,0:T(4,128)S(1)}, u32[]{:S(2)}) copy-start(f32[4,256]{1,0:T(4,128)S(1)} %get-tuple-element.33) | copy-start | bytes 12292
  14.1 255.5 %all-gather.5.cloned.1.call-start = ((), (), s32[]{:S(2)}) async-start(), calls=%async_computation.16 | async-start | bytes 4718592 | tf_op jit(solution)/shard_map/all_gather | solution.py:100
  18.3 299.2 %all-gather.11.cloned.1.call-start = ((), (), s32[]{:S(2)}) async-start(), calls=%async_computation.19 | async-start | bytes 4718592 | tf_op jit(solution)/shard_map/all_gather | solution.py:99
  23.3 327.6 %all-gather.9.cloned.1.call-start = ((), (), s32[]{:S(2)}) async-start(), calls=%async_computation.18 | async-start | bytes 4718592 | tf_op jit(solution)/shard_map/all_gather | solution.py:100
  26.0 537.0 %reduce-scatter.41.cloned.1.call-start = ((), (), s32[]{:S(2)}) async-start(), calls=%async_computation.27 | async-start | bytes 2506752 | tf_op jit(solution)/shard_map/reduce_scatter | solution.py:200
  34.5 14.9 %copy-start.18 = (s32[256,512]{0,1:T(8,128)}, s32[256,512]{0,1:T(8,128)S(1)}, u32[]{:S(2)}) copy-start(s32[256,512]{0,1:T(8,128)S(1)} %fusion.112) | copy-start | bytes 1572868
  287.0 15.7 %slice-start.3 = ((s8[4718592]{0:T(1024)(128)(4,1)}), s8[4194304]{0:T(1024)(128)(4,1)S(1)}, s32[]{:S(2)}) async-start(s8[4718592]{0:T(1024)(128)(4,1)} %bitcast.241), calls=%async_computation.39 | async-start | bytes 8388608
  290.6 41.7 %copy-start.37 = (f32[4,256]{1,0:T(4,128)}, f32[4,256]{1,0:T(4,128)S(1)}, u32[]{:S(2)}) copy-start(f32[4,256]{1,0:T(4,128)S(1)} %get-tuple-element.35) | copy-start | bytes 12292
  364.2 36.8 %copy-start.4 = (f32[8,128,768]{2,1,0:T(8,128)}, f32[8,128,768]{2,1,0:T(8,128)S(1)}, u32[]{:S(2)}) copy-start(f32[8,128,768]{2,1,0:T(8,128)S(1)} %get-tuple-element.43) | copy-start | bytes 9437188
  364.2 36.8 %copy-start.35 = (f32[8,128]{1,0:T(8,128)}, f32[8,128]{1,0:T(8,128)S(1)}, u32[]{:S(2)}) copy-start(f32[8,128]{1,0:T(8,128)S(1)} %get-tuple-element.31) | copy-start | bytes 12292
  415.0 263.9 %reduce-scatter.35.cloned.1.call-start = ((), (), s32[]{:S(2)}) async-start(), calls=%async_computation.24 | async-start | bytes 2506752 | tf_op jit(solution)/shard_map/reduce_scatter | solution.py:200
  438.8 25.1 %copy-start.2 = (bf16[4,512,768]{1,2,0:T(8,128)(2,1)S(1)}, bf16[4,512,768]{1,2,0:T(8,128)(2,1)}, u32[]{:S(2)}) copy-start(bf16[4,512,768]{1,2,0:T(8,128)(2,1)} %copy.102) | copy-start | bytes 9437188
  509.3 181.9 %reduce-scatter.29.cloned.1.call-start = ((), (), s32[]{:S(2)}) async-start(), calls=%async_computation.21 | async-start | bytes 4718592 | tf_op jit(solution)/shard_map/reduce_scatter | solution.py:173
  526.0 179.6 %reduce-scatter.33.cloned.1.call-start = ((), (), s32[]{:S(2)}) async-start(), calls=%async_computation.23 | async-start | bytes 4718592 | tf_op jit(solution)/shard_map/reduce_scatter | solution.py:173
  538.2 181.7 %reduce-scatter.27.cloned.1.call-start = ((), (), s32[]{:S(2)}) async-start(), calls=%async_computation.20 | async-start | bytes 4718592 | tf_op jit(solution)/shard_map/reduce_scatter | solution.py:170
  552.2 182.1 %reduce-scatter.31.cloned.1.call-start = ((), (), s32[]{:S(2)}) async-start(), calls=%async_computation.22 | async-start | bytes 4718592 | tf_op jit(solution)/shard_map/reduce_scatter | solution.py:170
  562.9 273.3 %reduce-scatter.55.cloned.1.call-start = ((), (), s32[]{:S(2)}) async-start(), calls=%async_computation.34 | async-start | bytes 294912
  564.8 273.0 %reduce-scatter.49.cloned.1.call-start = ((), (), s32[]{:S(2)}) async-start(), calls=%async_computation.31 | async-start | bytes 294912
  680.6 210.9 %reduce-scatter.39.cloned.1.call-start = ((), (), s32[]{:S(2)}) async-start(), calls=%async_computation.26 | async-start | bytes 2506752 | tf_op jit(solution)/shard_map/reduce_scatter | solution.py:200
  710.8 313.8 %reduce-scatter.37.cloned.1.call-start = ((), (), s32[]{:S(2)}) async-start(), calls=%async_computation.25 | async-start | bytes 2506752 | tf_op jit(solution)/shard_map/reduce_scatter | solution.py:200
  739.5 461.5 %reduce-scatter.47.cloned.1.call-start = ((), (), s32[]{:S(2)}) async-start(), calls=%async_computation.30 | async-start | bytes 10027008 | tf_op jit(solution)/shard_map/reduce_scatter | solution.py:200
  763.0 614.5 %reduce-scatter.43.cloned.1.call-start = ((), (), s32[]{:S(2)}) async-start(), calls=%async_computation.28 | async-start | bytes 10027008 | tf_op jit(solution)/shard_map/reduce_scatter | solution.py:200
  782.7 603.4 %reduce-scatter.53.cloned.1.call-start = ((), (), s32[]{:S(2)}) async-start(), calls=%async_computation.33 | async-start | bytes 294912
  795.9 13.4 copy-start.28
  795.9 19.8 %slice-start.5 = ((s8[4718592]{0:T(1024)(128)(4,1)}), s8[4194304]{0:T(1024)(128)(4,1)S(1)}, s32[]{:S(2)}) async-start(s8[4718592]{0:T(1024)(128)(4,1)} %bitcast.243), calls=%async_computation.41 | async-start | bytes 8388608
  812.6 14.9 %slice-start.7 = ((s8[12582912]{0:T(1024)(128)(4,1)}), s8[4194304]{0:T(1024)(128)(4,1)S(1)}, s32[]{:S(2)}) async-start(s8[12582912]{0:T(1024)(128)(4,1)} %bitcast.247), calls=%async_computation.43 | async-start | bytes 8388608
  893.3 504.2 %reduce-scatter.51.cloned.1.call-start = ((), (), s32[]{:S(2)}) async-start(), calls=%async_computation.32 | async-start | bytes 294912
  1026.4 176.7 %copy-start.47 = (f32[8,128]{1,0:T(8,128)S(1)}, f32[8,128]{1,0:T(8,128)}, u32[]{:S(2)}) copy-start(f32[8,128]{1,0:T(8,128)} %get-tuple-element.28) | copy-start | bytes 12292
  1026.4 382.4 %reduce-scatter.57.cloned.1.call-start = ((), (), s32[]{:S(2)}) async-start(), calls=%async_computation.35 | async-start | bytes 589824
  1203.0 217.3 %reduce-scatter.45.cloned.1.call-start = ((), (), s32[]{:S(2)}) async-start(), calls=%async_computation.29 | async-start | bytes 442368 | tf_op jit(solution)/shard_map/reduce_scatter | solution.py:203
  1203.1 176.3 %copy-start.46 = (f32[4,256]{1,0:T(4,128)S(1)}, f32[4,256]{1,0:T(4,128)}, u32[]{:S(2)}) copy-start(f32[4,256]{1,0:T(4,128)} %get-tuple-element.32) | copy-start | bytes 12292
  (54 other events, 379.8 us)
Sparse Core Ops, SparseCore 0:
  14.2 14.8 all-gather.6
  31.2 13.2 all-gather.4
  46.1 13.2 all-gather.10
  60.8 13.2 all-gather.8
  415.1 130.8 reduce-scatter.40
  551.5 127.3 reduce-scatter.34
  681.1 10.0 reduce-scatter.28
  693.5 12.0 reduce-scatter.32
  707.9 12.0 reduce-scatter.26
  722.1 12.0 reduce-scatter.30
  737.1 8.7 reduce-scatter.54
  748.5 8.7 reduce-scatter.48
  762.2 129.3 reduce-scatter.38
  897.1 127.4 reduce-scatter.36
  1030.1 170.8 reduce-scatter.46
  1207.5 169.9 reduce-scatter.42
  1379.6 6.4 reduce-scatter.52
  1388.7 8.7 reduce-scatter.50
  1399.7 8.9 reduce-scatter.56
  1411.5 8.8 reduce-scatter.44
where the time goes:
time: 1440 us; the launch traced here: 1430 us
  waiting for transfers between devices  652 us (45%)
  matrix products  377 us (26%)
  local copies, waits for them, and re-layouts  276 us (19%)
  other arithmetic  65.5 us (5%)
  blocking collectives  41.6 us (3%)
  between operations  15.3 us (1%)
    reduce_scatter x6, waiting for transfers between devices, reduce_large(): lax.psum_scatter(large_part, 'rows', scatter_dimension=0, tiled=True)  582 us
    eq x2, local copies, waits for them, and re-layouts, layer_bucket(): bucket_ids(query_pos, key_pos, buckets)[None] == bucket_range  191 us
    dot_general x12, matrix products, back_project(): jnp.einsum('kyz,vz->kyv', gradient_half, weight_matrix, preferred_element...  80 us
    dot_general x12, matrix products, weight_grad(): jnp.einsum('hyk,hyg->kg', left_operand, right_operand, preferred_element_...  79.2 us
    dot_general x12, matrix products, project(): jnp.einsum('ung,gr->unr', left_operand, weight_matrix, preferred_element_...  70.1 us
    psum x1, blocking collectives, body(): lax.psum((small_local[0], small_local[1], small_local[2]), ('rows', 'seq'))  41.6 us
    reduce_sum x2, other arithmetic, layer_bucket(): jnp.einsum('rgtj,etj->eg', score_gradient, bucket_indicator, precision=to...  35.4 us
    dot_general x2, matrix products, layer_bucket(): jnp.einsum('sqhe,skhe->shqk', d_attn_heads, to_heads(values_back, full_le...  34.2 us
  transfers between devices with their start and end apart: 20, of which 13 were waited for; matrix products, arithmetic and copies ran while one was open for 45% of the time, Pallas kernels for 0%

commit v1 on v0

v1 whole, which is shorter than its diff:
```python
import functools

import jax
import jax.numpy as jnp
from jax import lax
from jax.experimental import pallas as pl
from jax.experimental.pallas import tpu as pltpu
from jax.sharding import PartitionSpec as P

EPS = 1e-06
EDGES = (12, 16, 23, 32, 46, 64, 91)
MASKED = -1e30
C1 = 0.7978845608
C3 = 0.044715
BF = jnp.bfloat16
F32 = jnp.float32
HEAD = 64
PAIR = 2 * HEAD
MIB = 1 << 20


def dot(a, b, ca, cb):
    return lax.dot_general(a, b, (((ca,), (cb,)), ((), ())), preferred_element_type=F32)


def exact(a, b):
    return lax.dot_general(
        a, b, (((1,), (0,)), ((), ())), precision=lax.Precision.HIGHEST, preferred_element_type=F32
    )


def sds(shape, dtype):
    return jax.ShapeDtypeStruct(shape, dtype)


def call(kernel, grid, in_specs, out_specs, out_shape, scratch=(), flops=0, nbytes=0, vmem=60):
    return pl.pallas_call(
        kernel,
        grid_spec=pltpu.PrefetchScalarGridSpec(
            num_scalar_prefetch=1,
            grid=grid,
            in_specs=in_specs,
            out_specs=out_specs,
            scratch_shapes=list(scratch),
        ),
        out_shape=out_shape,
        compiler_params=pltpu.CompilerParams(vmem_limit_bytes=vmem * MIB),
        cost_estimate=pl.CostEstimate(flops=int(flops), bytes_accessed=int(nbytes), transcendentals=0),
    )


def whole(shape):
    return pl.BlockSpec(shape, lambda *_: (0,) * len(shape))


def bucket_of(rel, buckets):
    n = jnp.abs(rel)
    far = jnp.full(rel.shape, 8, jnp.int32)
    for edge in EDGES:
        far = far + (n >= edge).astype(jnp.int32)
    return jnp.where(n < 8, n, far) + jnp.where(rel > 0, buckets // 2, 0)


def strip_kernel(meta, table, strip, *, base, buckets, head_count):
    rows = strip.shape[1]
    rel = lax.broadcasted_iota(jnp.int32, (rows, 128), 0) - base - lax.broadcasted_iota(jnp.int32, (rows, 128), 1)
    ids = bucket_of(rel, buckets)
    h = pl.program_id(0)
    acc = jnp.zeros((rows, 128), F32)
    for b in range(buckets):
        acc = jnp.where(ids == b, table[b, h], acc)
    strip[0] = acc


def qkv_kernel(meta, x_ref, gain, wq, wk, wv, normed, q, k, v):
    x = x_ref[0].astype(F32)
    r = lax.rsqrt(jnp.mean(x * x, axis=-1, keepdims=True) + EPS)
    n = (x * r * gain[...]).astype(BF)
    normed[0] = n
    q[0] = dot(n, wq[...], 1, 0).astype(BF)
    k[0] = dot(n, wk[...], 1, 0).astype(BF)
    v[0] = dot(n, wv[...], 1, 0).astype(BF)


def units_of(na, la, nb, lb):
    out = [(0, s, la, s * la // 2) for s in range(na)]
    return out + [(1, s, lb, na * la // 2 + s * lb // 2) for s in range(nb)]


def joined(ref, off, half):
    return jnp.concatenate([ref[0, off : off + half, :], ref[1, off : off + half, :]], axis=0)


def strip_rows(flip, base, size, cb, kh):
    half = size // 2
    plain = base - 128 * cb + half * kh
    if flip is None:
        return plain
    moved = (128 * cb + half) % size
    return pl.multiple_of(jnp.where(flip == 0, plain, base - moved + half * (1 - kh)), 128)


def lanes_of(shape, high):
    lane = lax.broadcasted_iota(jnp.int32, shape, len(shape) - 1)
    return (lane >= HEAD) == high


def half_mask(high):
    return jnp.where(lanes_of((1, PAIR), high), 1.0, 0.0).astype(BF)


def attn_kernel(meta, q, k, v, strip, pa, pb, attn, kaug, *, dims, base):
    na, la, nb, lb = dims
    flip = meta[0]

    @pl.when(pl.program_id(0) == 0)
    def _():
        for kind, s, size, off in units_of(*dims):
            half = size // 2
            for kh in range(2):
                row = lax.broadcasted_iota(jnp.int32, (half, 128), 0)
                start = jnp.where(flip == 0, half * kh, half * (1 - kh))
                length = meta[2 + (s if kind == 0 else na + s)]
                lane = lax.broadcasted_iota(jnp.int32, (half, 128), 1)
                gone = jnp.logical_and(row + start >= length, lane == 0)
                kaug[kh, off : off + half, :] = jnp.where(gone, MASKED, 0.0).astype(BF)

    for kind, s, size, off in units_of(*dims):
        half = size // 2
        pref = pa if kind == 0 else pb
        q2, k2, v2 = joined(q, off, half), joined(k, off, half), joined(v, off, half)
        v2t = v2.T
        ones = jnp.where(lax.broadcasted_iota(jnp.int32, (size, 128), 1) == 0, 1.0, 0.0).astype(BF)
        qa = jnp.concatenate([q2, ones], axis=1)
        ka = joined(kaug, off, half)
        mixed = []
        for h in range(2):
            kk = jnp.concatenate([k2 * half_mask(h == 1), ka], axis=1)
            for c2 in range(size // 256):
                scores = dot(kk, qa[256 * c2 : 256 * c2 + 256], 1, 1)
                for sub in range(2):
                    cb = 2 * c2 + sub
                    bias = jnp.concatenate(
                        [strip[h, pl.ds(strip_rows(flip, base, size, cb, kh), half), :] for kh in range(2)], axis=0
                    )
                    one = scores[:, 128 * sub : 128 * sub + 128] + bias
                    e = jnp.exp(one - jnp.max(one, axis=0, keepdims=True))
                    p = e * (1.0 / jnp.sum(e, axis=0, keepdims=True))
                    pref[h, s, :, 128 * cb : 128 * cb + 128] = p.astype(BF)
            mixed.append(dot(v2t[HEAD * h : HEAD * h + HEAD], pref[h, s], 1, 0))
        o = jnp.concatenate(mixed, axis=0).T.astype(BF)
        attn[0, off : off + half, :] = o[:half]
        attn[1, off : off + half, :] = o[half:]


def mix_kernel(meta, attn, x, w_out, gain, hidden, normed):
    h = x[0].astype(F32) + dot(attn[0], w_out[...], 1, 0)
    r = lax.rsqrt(jnp.mean(h * h, axis=-1, keepdims=True) + EPS)
    hidden[0] = h
    normed[0] = (h * r * gain[...]).astype(BF)


def ffn_kernel(meta, normed, g, w_in, w_back, low, d_inner, *, step):
    for part in range(2):
        for lo in range(0, normed.shape[1], step):
            rows = slice(lo, lo + step)
            v = dot(normed[part, rows, :], w_in[...], 1, 0)
            gw = dot(g[part, rows, :], w_back[...], 1, 1)
            u = v * v
            t = jnp.tanh(v * (C1 + (C1 * C3) * u))
            up = 0.5 + 0.5 * t
            low[part, rows, :] = (v * up).astype(BF)
            slope = up + v * (0.5 - 0.5 * (t * t)) * (C1 + (3.0 * C1 * C3) * u)
            d_inner[part, rows, :] = (gw * slope).astype(BF)


def flat(ref):
    a = ref[...]
    return a.reshape(a.shape[0] * a.shape[1], a.shape[2])


def split_columns(meta, value, send, keep):
    half = value.shape[1] // 2
    lo, hi = value[:, :half].astype(BF), value[:, half:].astype(BF)
    first = meta[1] == 0

    @pl.when(first)
    def _():
        keep[...] = lo
        send[...] = hi

    @pl.when(jnp.logical_not(first))
    def _():
        keep[...] = hi
        send[...] = lo


def back_grad_kernel(meta, low, g, send, keep):
    split_columns(meta, dot(flat(low), flat(g), 0, 0), send, keep)


def in_grad_kernel(meta, normed, d_inner, send, keep):
    value = dot(flat(normed), flat(d_inner), 0, 0).astype(BF)
    sending = pl.program_id(0) < pl.num_programs(0) // 2

    @pl.when(sending)
    def _():
        send[...] = value

    @pl.when(jnp.logical_not(sending))
    def _():
        keep[...] = value


def rows8(value):
    return jnp.sum(value.reshape(value.shape[0] // 8, 8, value.shape[1]), axis=0)


def hidden_kernel(meta, d_inner, w_in, hidden, g, gain, w_out, attn, d_hidden, d_attn, small, send, keep, acc):
    i, last = pl.program_id(0), pl.num_programs(0) - 1
    dn = dot(d_inner[0], w_in[...], 1, 1)
    h = hidden[0]
    r = lax.rsqrt(jnp.mean(h * h, axis=-1, keepdims=True) + EPS)
    gained = dn * gain[...]
    mean = jnp.mean(gained * h, axis=-1, keepdims=True)
    dh = (g[0].astype(F32) + r * gained - h * (r * r * r * mean)).astype(BF)
    d_hidden[0] = dh
    d_attn[0] = dot(dh, w_out[...], 1, 1).astype(BF)
    part = rows8(dn * h * r)
    product = dot(attn[0], dh, 0, 0)

    @pl.when(i == 0)
    def _():
        small[...] = part
        acc[...] = product

    @pl.when(i > 0)
    def _():
        small[...] += part
        acc[...] += product

    @pl.when(i == last)
    def _():
        split_columns(meta, acc[...], send, keep)


def table_sums(acc, base, buckets):
    near0, near1 = base - 96, base + 224
    near = acc[near0:near1, :]
    rel = (near0 - base) + lax.broadcasted_iota(jnp.int32, near.shape, 0) - lax.broadcasted_iota(jnp.int32, near.shape, 1)
    far_plus = jnp.sum(acc[near1:, :], axis=0, keepdims=True) + jnp.sum(
        jnp.where(rel >= 128, near, 0.0), axis=0, keepdims=True
    )
    far_minus = jnp.sum(acc[:near0, :], axis=0, keepdims=True) + jnp.sum(
        jnp.where(rel <= -128, near, 0.0), axis=0, keepdims=True
    )
    inner = jnp.where(jnp.abs(rel) < 128, near, 0.0)
    lanes = (128, 128)
    mirror = lax.broadcasted_iota(jnp.int32, lanes, 0) + lax.broadcasted_iota(jnp.int32, lanes, 1) == 127
    inner = exact(inner, mirror.astype(F32))
    wide = jnp.concatenate([inner, jnp.zeros_like(inner)], axis=1)
    turned = pltpu.roll(wide, 0, 1, stride=1, stride_axis=0)
    line = jnp.sum(turned, axis=0, keepdims=True)
    lane = lax.broadcasted_iota(jnp.int32, (256, 128), 0)
    back = ((lane + near0 - base - 127 + 128 + 512) & 255) - 128
    hot = jnp.logical_and(
        bucket_of(back, buckets) == lax.broadcasted_iota(jnp.int32, (256, 128), 1), back > -128
    ).astype(F32)
    sums = exact(jnp.broadcast_to(line, (8, 256)), hot)[:1]
    out = lax.broadcasted_iota(jnp.int32, (1, 128), 1)
    sums = sums + jnp.where(out == buckets - 1, jnp.sum(far_plus, axis=1, keepdims=True), 0.0)
    return sums + jnp.where(out == buckets // 2 - 1, jnp.sum(far_minus, axis=1, keepdims=True), 0.0)


def attn_back_kernel(
    meta, q, k, v, do, pa, pb, normed, dq, dk, dv, table, send, keep, strip, dsa, dsb, cat, *, dims, base, buckets
):
    flip = meta[0]
    step = pl.program_id(0)
    th = normed.shape[1]
    strip[...] = jnp.zeros_like(strip)
    for kind, s, size, off in units_of(*dims):
        half = size // 2
        pref = pa if kind == 0 else pb
        ds_ref = dsa if kind == 0 else dsb
        q2, k2, v2, o2 = (joined(ref, off, half) for ref in (q, k, v, do))
        k2t = k2.T
        dvs, dks, dqs = [], [], []
        for h in range(2):
            mask = half_mask(h == 1)
            vm = v2 * mask
            for c2 in range(size // 256):
                dp = dot(vm, o2[256 * c2 : 256 * c2 + 256], 1, 1)
                for sub in range(2):
                    cb = 2 * c2 + sub
                    cols = slice(128 * cb, 128 * cb + 128)
                    p = pref[h, s, :, cols].astype(F32)
                    dpc = dp[:, 128 * sub : 128 * sub + 128]
                    delta = jnp.sum(p * dpc, axis=0, keepdims=True)
                    ds = p * (dpc - delta)
                    for kh in range(2):
                        at = pl.ds(strip_rows(flip, base, size, cb, kh), half)
                        strip[h, at, :] += ds[half * kh : half * kh + half]
                    ds_ref[:, cols] = ds.astype(BF)
            dvs.append(dot(pref[h, s], o2 * mask, 1, 0))
            dks.append(dot(ds_ref[...], q2 * mask, 1, 0))
            dqs.append(dot(k2t[HEAD * h : HEAD * h + HEAD], ds_ref[...], 1, 0))
        d_v = (dvs[0] + dvs[1]).astype(BF)
        d_k = (dks[0] + dks[1]).astype(BF)
        d_q = jnp.concatenate(dqs, axis=0).T.astype(BF)
        for part in range(2):
            rows = slice(off, off + half)
            got = slice(part * half, part * half + half)
            dq[part, rows, :] = d_q[got]
            dk[part, rows, :] = d_k[got]
            dv[part, rows, :] = d_v[got]
            at = slice(part * th + off, part * th + off + half)
            cat[step, at, 0:128] = d_q[got]
            cat[step, at, 128:256] = d_k[got]
            cat[step, at, 256:384] = d_v[got]
    rows = [table_sums(strip.at[h], base, buckets) for h in range(2)]
    table[0] = jnp.concatenate(rows + [jnp.zeros((6, 128), F32)], axis=0)

    @pl.when(step == 1)
    def _():
        both = jnp.concatenate([cat[0], cat[1]], axis=1)
        value = dot(flat(normed), both, 0, 0).astype(BF)
        send[...] = value[:, :384]
        keep[...] = value[:, 384:]


def out_kernel(meta, low, w_back, hidden, out):
    out[0] = (hidden[0] + dot(low[0], w_back[...], 1, 0)).astype(BF)


def tokens_kernel(meta, dq, dk, dv, wq, wk, wv, x_ref, d_hidden, gain, grad, small):
    i = pl.program_id(0)
    dn = dot(dq[0], wq[...], 1, 1) + dot(dk[0], wk[...], 1, 1) + dot(dv[0], wv[...], 1, 1)
    x = x_ref[0].astype(F32)
    r = lax.rsqrt(jnp.mean(x * x, axis=-1, keepdims=True) + EPS)
    gained = dn * gain[...]
    mean = jnp.mean(gained * x, axis=-1, keepdims=True)
    grad[0] = (d_hidden[0].astype(F32) + r * gained - x * (r * r * r * mean)).astype(BF)
    part = rows8(dn * x * r)

    @pl.when(i == 0)
    def _():
        small[...] = part

    @pl.when(i > 0)
    def _():
        small[...] += part


def swap(x, axis, bit):
    n = lax.axis_size(axis)
    return lax.ppermute(x, axis, [(i, i ^ bit) for i in range(n)])


def halve(x, bit_pos):
    bit = (lax.axis_index("rows") >> bit_pos) & 1
    axis = x.ndim - 3 - bit_pos
    mine = lax.dynamic_index_in_dim(x, bit, axis, keepdims=True)
    other = lax.dynamic_index_in_dim(x, 1 - bit, axis, keepdims=True)
    got = swap(other, "rows", 1 << bit_pos)
    return mine.astype(F32) + got.astype(F32)


def scatter_rows(x, order):
    n = lax.axis_size("rows")
    bits = n.bit_length() - 1
    x = x.reshape((2,) * bits + (x.shape[0] // n, x.shape[1]))
    for i, b in enumerate(order):
        x = halve(x, b)
        if i < bits - 1:
            x = x.astype(BF)
    return x.reshape(x.shape[-2:])


def body(
    tokens_a, lengths_a, cotangent_a, tokens_b, lengths_b, cotangent_b,
    gain_attn, w_query, w_key, w_value, w_out, relative_bias_table, gain_ffn, w_in, w_back,
):
    nseq, nrows = lax.axis_size("seq"), lax.axis_size("rows")
    c = lax.axis_index("seq")
    width = tokens_a.shape[2]
    ff = w_in.shape[1]
    buckets, head_count = relative_bias_table.shape
    la, lb = tokens_a.shape[1] * nseq, tokens_b.shape[1] * nseq
    na, nb = tokens_a.shape[0] // nseq, tokens_b.shape[0] // nseq
    dims = (na, la, nb, lb)
    th = (na * la + nb * lb) // 2
    tokens = 2 * th
    base = la - 128
    strip_len = 2 * la - 128
    pairs = head_count // 2
    paired = nseq == 2

    if paired:
        me = c
        flip = c

        def regroup(a, b):
            def pick(x, n, which):
                got = lax.dynamic_slice_in_dim(x, which * n, n, 0)
                return got.reshape(-1, width)

            own = jnp.concatenate([pick(a, na, c), pick(b, nb, c)], axis=0)
            give = jnp.concatenate([pick(a, na, 1 - c), pick(b, nb, 1 - c)], axis=0)
            return jnp.stack([own, swap(give, "seq", 1)])

        def ungroup(x):
            own, got = x[0], swap(x[1], "seq", 1)
            cut = na * la // 2
            first = c == 0

            def place(o, g, n, size):
                o, g = o.reshape(n, size, width), g.reshape(n, size, width)
                return jnp.concatenate([jnp.where(first, o, g), jnp.where(first, g, o)], axis=0)

            return place(own[:cut], got[:cut], na, la // 2), place(own[cut:], got[cut:], nb, lb // 2)

    else:
        me = jnp.int32(0)
        flip = jnp.int32(0)

        def regroup(a, b):
            def one(x):
                got = lax.all_to_all(x, "seq", 0, 1, tiled=True)
                n, size, _ = got.shape
                return got.reshape(n, 2, size // 2, width).transpose(1, 0, 2, 3).reshape(2, -1, width)

            return jnp.concatenate([one(a), one(b)], axis=1)

        def ungroup(x):
            cut = na * la // 2

            def one(y, n, size):
                y = y.reshape(2, n, size // 2, width).transpose(1, 0, 2, 3).reshape(n, size, width)
                return lax.all_to_all(y, "seq", 1, 0, tiled=True)

            return one(x[:, :cut], na, la), one(x[:, cut:], nb, lb)

    own_a = lax.dynamic_slice_in_dim(lengths_a, c * na, na, 0)
    own_b = lax.dynamic_slice_in_dim(lengths_b, c * nb, nb, 0)
    meta = jnp.concatenate([jnp.stack([flip, me]).astype(jnp.int32), own_a, own_b])
    x = regroup(tokens_a, tokens_b)
    g = regroup(cotangent_a, cotangent_b)
    gain1, gain2 = gain_attn[None], gain_ffn[None]

    tile = min(512, th)
    per = th // tile
    row_grid = (2 * per,)
    by_row = lambda w: pl.BlockSpec((1, tile, w), lambda i, m: (i // per, i % per, 0))
    dense = 2 * tokens * width

    strip = call(
        functools.partial(strip_kernel, base=base, buckets=buckets, head_count=head_count),
        (head_count,),
        [pl.BlockSpec(memory_space=pltpu.SMEM)],
        pl.BlockSpec((1, strip_len, 128), lambda h, m: (h, 0, 0)),
        sds((head_count, strip_len, 128), F32),
        flops=1e9,
        nbytes=4 * head_count * strip_len * 128,
    )(meta, relative_bias_table)

    tok = sds((2, th, width), BF)
    normed, q, k, v = call(
        qkv_kernel,
        row_grid,
        [by_row(width), whole((1, width))] + [whole((width, width))] * 3,
        [by_row(width)] * 4,
        [tok] * 4,
        flops=3 * dense * width,
        nbytes=10 * tokens * width,
    )(meta, x, gain1, w_query, w_key, w_value)

    by_pair = pl.BlockSpec((2, th, PAIR), lambda p, m: (0, 0, p))
    pa_shape, pb_shape = (head_count, na, la, la), (head_count, nb, lb, lb)
    score_macs = head_count * (na * la * la + nb * lb * lb)
    pa, pb, attn = call(
        functools.partial(attn_kernel, dims=dims, base=base),
        (pairs,),
        [by_pair] * 3 + [pl.BlockSpec((2, strip_len, 128), lambda p, m: (p, 0, 0))],
        [
            pl.BlockSpec((2, na, la, la), lambda p, m: (p, 0, 0, 0)),
            pl.BlockSpec((2, nb, lb, lb), lambda p, m: (p, 0, 0, 0)),
            by_pair,
        ],
        [sds(pa_shape, BF), sds(pb_shape, BF), tok],
        scratch=[pltpu.VMEM((2, th, 128), BF)],
        flops=score_macs * 256 * 4,
        nbytes=2 * score_macs,
    )(meta, q, k, v, strip)

    hidden, normed2 = call(
        mix_kernel,
        row_grid,
        [by_row(width), by_row(width), whole((width, width)), whole((1, width))],
        [by_row(width)] * 2,
        [sds((2, th, width), F32), tok],
        flops=dense * width,
        nbytes=10 * tokens * width,
    )(meta, attn, x, w_out, gain2)

    all_tok = whole((2, th, width))
    fb = 512
    by_ff = pl.BlockSpec((2, th, fb), lambda f, m: (0, 0, f))
    wide = sds((2, th, ff), BF)
    low, d_inner = call(
        functools.partial(ffn_kernel, step=min(512, th)),
        (ff // fb,),
        [
            all_tok,
            all_tok,
            pl.BlockSpec((width, fb), lambda f, m: (0, f)),
            pl.BlockSpec((fb, width), lambda f, m: (f, 0)),
        ],
        [by_ff, by_ff],
        [wide, wide],
        flops=2 * dense * ff,
        nbytes=4 * tokens * ff,
    )(meta, normed2, g, w_in, w_back)

    half_w, half_f = width // 2, ff // 2
    back_send, back_keep = call(
        back_grad_kernel,
        (ff // fb,),
        [by_ff, all_tok],
        [pl.BlockSpec((fb, half_w), lambda f, m: (f, 0))] * 2,
        [sds((ff, half_w), BF)] * 2,
        flops=dense * ff,
        nbytes=2 * tokens * ff,
    )(meta, low, g)

    nf = ff // fb
    in_send, in_keep = call(
        in_grad_kernel,
        (nf,),
        [all_tok, pl.BlockSpec((2, th, fb), lambda f, m: (0, 0, (f + (1 - m[1]) * (nf // 2)) % nf))],
        [
            pl.BlockSpec((width, fb), lambda f, m: (0, jnp.minimum(f, nf // 2 - 1))),
            pl.BlockSpec((width, fb), lambda f, m: (0, jnp.maximum(f - nf // 2, 0))),
        ],
        [sds((width, half_f), BF)] * 2,
        flops=dense * ff,
        nbytes=2 * tokens * ff,
    )(meta, normed2, d_inner)

    small = sds((8, width), F32)
    d_hidden, d_attn, small_ffn, out_send, out_keep = call(
        hidden_kernel,
        row_grid,
        [
            by_row(ff),
            whole((width, ff)),
            by_row(width),
            by_row(width),
            whole((1, width)),
            whole((width, width)),
            by_row(width),
        ],
        [by_row(width), by_row(width), whole((8, width)), whole((width, half_w)), whole((width, half_w))],
        [tok, tok, small, sds((width, half_w), BF), sds((width, half_w), BF)],
        scratch=[pltpu.VMEM((width, width), F32)],
        flops=dense * (ff + 2 * width),
        nbytes=2 * tokens * ff,
    )(meta, d_inner, w_in, hidden, g, gain2, w_out, attn)

    def seq_sum(send, keep, dim):
        if paired:
            return (keep.astype(F32) + swap(send, "seq", 1).astype(F32)).astype(BF)
        return jnp.concatenate([keep, send], axis=dim)

    back_part = seq_sum(back_send, back_keep, 1)
    in_part = seq_sum(in_send, in_keep, 1)
    out_part = seq_sum(out_send, out_keep, 1)

    group_count = pairs // 2
    groups, dqs, tables = [], [], []
    for gi in range(group_count):

        def pair_at(s, m, gi=gi):
            return jnp.where(s == 0, 1 - m[1], m[1]) * group_count + gi

        def half_at(s, m):
            return jnp.where(s == 0, 1 - m[1], m[1])

        by_cols = pl.BlockSpec((2, th, PAIR), lambda s, m, f=pair_at: (0, 0, f(s, m)))
        to_cols = pl.BlockSpec((2, th, PAIR), lambda s, m: (0, 0, half_at(s, m)))
        dq, dk, dv, table, send, keep = call(
            functools.partial(attn_back_kernel, dims=dims, base=base, buckets=buckets),
            (2,),
            [by_cols] * 4
            + [
                pl.BlockSpec((2, na, la, la), lambda s, m, f=pair_at: (f(s, m), 0, 0, 0)),
                pl.BlockSpec((2, nb, lb, lb), lambda s, m, f=pair_at: (f(s, m), 0, 0, 0)),
                all_tok,
            ],
            [to_cols] * 3
            + [
                pl.BlockSpec((1, 8, 128), lambda s, m: (half_at(s, m), 0, 0)),
                whole((width, 3 * PAIR)),
                whole((width, 3 * PAIR)),
            ],
            [sds((2, th, 2 * PAIR), BF)] * 3
            + [sds((2, 8, 128), F32), sds((width, 3 * PAIR), BF), sds((width, 3 * PAIR), BF)],
            scratch=[
                pltpu.VMEM((2, strip_len, 128), F32),
                pltpu.VMEM((la, la), BF),
                pltpu.VMEM((lb, lb), BF),
                pltpu.VMEM((2, tokens, 3 * PAIR), BF),
            ],
            flops=score_macs * 256 * 8 // 3 + dense * width,
            nbytes=2 * score_macs // 3,
        )(meta, q, k, v, d_attn, pa, pb, normed)
        dqs.append((dq, dk, dv))
        tables.append(table)
        if paired:
            groups.append(seq_sum(send, keep, 1))
        else:
            groups.append((keep, send))

    out_parts = call(
        out_kernel,
        row_grid,
        [by_row(ff), whole((ff, width)), by_row(width)],
        by_row(width),
        tok,
        flops=dense * ff,
        nbytes=2 * tokens * ff,
    )(meta, low, w_back, hidden)
    out_a, out_b = ungroup(out_parts)

    def joined_cols(which):
        pieces = [d[which] for d in dqs]
        return jnp.concatenate([p[:, :, :PAIR] for p in pieces] + [p[:, :, PAIR:] for p in pieces], axis=2)

    grads, small_attn = call(
        tokens_kernel,
        row_grid,
        [by_row(width)] * 3 + [whole((width, width))] * 3 + [by_row(width), by_row(width), whole((1, width))],
        [by_row(width), whole((8, width))],
        [tok, small],
        flops=3 * dense * width,
        nbytes=14 * tokens * width,
    )(meta, joined_cols(0), joined_cols(1), joined_cols(2), w_query, w_key, w_value, x, d_hidden, gain1)
    grad_a, grad_b = ungroup(grads)

    table_local = jnp.stack([t[:, :2, :buckets] for t in tables], axis=1).reshape(head_count, buckets).T
    gain_one, table_sum, gain_two = lax.psum(
        (jnp.sum(small_attn, axis=0), table_local, jnp.sum(small_ffn, axis=0)), ("rows", "seq")
    )

    if paired:
        bits = nrows.bit_length() - 1
        orders = [tuple(range(bits)), (1, 0) + tuple(range(2, bits))]
        g_back = jnp.concatenate(
            [scatter_rows(back_part[:, s], o) for s, o in zip((slice(0, 128), slice(128, None)), orders)], axis=1
        )
        g_in = jnp.concatenate(
            [scatter_rows(in_part[:, s], o) for s, o in zip((slice(0, 768), slice(768, None)), orders)], axis=1
        )
        g_out = scatter_rows(out_part, orders[0])
        qkv = [scatter_rows(part, orders[i % 2]) for i, part in enumerate(groups)]
        g_q, g_k, g_v = (
            jnp.concatenate([part[:, PAIR * i : PAIR * i + PAIR] for part in qkv], axis=1) for i in range(3)
        )
    else:

        def reduce(x):
            x = lax.psum_scatter(x.astype(F32), "rows", scatter_dimension=0, tiled=True)
            return lax.psum_scatter(x.astype(BF), "seq", scatter_dimension=1, tiled=True).astype(F32)

        g_back, g_in, g_out = reduce(back_part), reduce(in_part), reduce(out_part)
        g_q, g_k, g_v = (
            reduce(
                jnp.concatenate([part[s][:, PAIR * i : PAIR * i + PAIR] for s in range(2) for part in groups], axis=1)
            )
            for i in range(3)
        )
    return (
        out_a, out_b, grad_a, grad_b, gain_one, g_q, g_k, g_v, g_out, table_sum, gain_two, g_in, g_back,
    )


def solution(mesh):
    split = P("rows", "seq", None)
    placed = (split, P("rows"), split, split, P("rows"), split) + (P(),) * 9
    shard = P("rows", "seq")
    return jax.shard_map(
        body,
        mesh=mesh,
        in_specs=placed,
        out_specs=(split, split, split, split, P(), shard, shard, shard, shard, P(), P(), shard, shard),
        check_vma=False,
    )
```

time: 1440 us -> 521 us (0.36)
  waiting for transfers between devices: 652 us -> 97.9 us
  matrix products: 377 us -> 0 us
  Pallas kernels: 0 us -> 266 us
  local copies, waits for them, and re-layouts: 276 us -> 25.2 us
  starting transfers between devices: 1.79 us -> 49 us
  other arithmetic: 65.5 us -> 29.9 us
    reduce_scatter x11 -> x0, waiting for transfers between devices: 630 us -> none  [the longest x6 582 us: reduce_large(): lax.psum_scatter(large_part, 'rows', scatter_dimension=0, tiled=True)]
    dot_general x50 -> x0, matrix products: 349 us -> none  [the longest x12 80 us: back_project(): jnp.einsum('kyz,vz->kyv', gradient_half, weight_matrix, preferred_element...]
    pallas_call x0 -> x13, Pallas kernels: none -> 266 us  [the longest x3 69.6 us: body(): call(functools.partial(attn_back_kernel, dims=dims, base=base, buckets=bu...]
    eq x2 -> x0, local copies, waits for them, and re-layouts: 191 us -> none  [layer_bucket(): bucket_ids(query_pos, key_pos, buckets)[None] == bucket_range]
    ppermute x0 -> x42, waiting for transfers between devices: none -> 97.9 us  [swap(): return lax.ppermute(x, axis, [(i, i ^ bit) for i in range(n)])]
    ppermute x0 -> x42, starting transfers between devices: none -> 49 us  [swap(): return lax.ppermute(x, axis, [(i, i ^ bit) for i in range(n)])]
    reduce_sum x4 -> x2, other arithmetic: 37.7 us -> 0.03 us  [the longest x1 0.01 us: body(): jnp.sum(small_attn, axis=0)]
    convert_element_type x8 -> x0, local copies, waits for them, and re-layouts: 29.3 us -> none  [the longest x2 9.41 us: layer_bucket(): value_part.astype(jnp.bfloat16)]
  transfers between devices with their start and end apart: 20 -> 42, of which waited for: 13 -> 27; matrix products, arithmetic and copies ran while one was open for 45% -> 6% of each run, Pallas kernels for 0% -> 3%
where the time goes in v1:
time: 521 us; the launch traced here: 513 us
  Pallas kernels  266 us (51%)
  waiting for transfers between devices  97.9 us (19%)
  starting transfers between devices  49 us (9%)
  blocking collectives  42 us (8%)
  other arithmetic  29.9 us (6%)
  local copies, waits for them, and re-layouts  25.2 us (5%)
    ppermute x42, waiting for transfers between devices, swap(): return lax.ppermute(x, axis, [(i, i ^ bit) for i in range(n)])  97.9 us
    pallas_call x3, Pallas kernels, body(): call(functools.partial(attn_back_kernel, dims=dims, base=base, buckets=bu...  69.6 us
    ppermute x42, starting transfers between devices, swap(): return lax.ppermute(x, axis, [(i, i ^ bit) for i in range(n)])  49 us
    psum x1, blocking collectives, body(): lax.psum((jnp.sum(small_attn, axis=0), table_local, jnp.sum(small_ffn, ax...  42 us
    pallas_call x1, Pallas kernels, body(): call(functools.partial(attn_kernel, dims=dims, base=base), (pairs,), [by_...  33.8 us
    pallas_call x1, Pallas kernels, body(): call(functools.partial(ffn_kernel, step=min(512, th)), (ff // fb,), [all_...  32.9 us
    pallas_call x1, Pallas kernels, body(): call(hidden_kernel, row_grid, [by_row(ff), whole((width, ff)), by_row(wid...  31.7 us
    pallas_call x1, Pallas kernels, body(): call(in_grad_kernel, (nf,), [all_tok, pl.BlockSpec((2, th, fb), lambda f,...  16 us
  transfers between devices with their start and end apart: 42, of which 27 were waited for; matrix products, arithmetic and copies ran while one was open for 6% of the time, Pallas kernels for 3%

profile of v1, /device:TPU:0, one launch (start us, length us, event | category | flops | bytes accessed | tf_op | source)
XLA Modules:
  0.0 512.6 jit_solution(13046756614637322190)
XLA Ops:
  9.4 13.5 %shard_map.247.strip = f32[12,896,128]{2,1,0:T(8,128)} custom-call(s32[8]{0:T(128)} %pad_add_fusion.meta, f32[32,12]{1,0:T(8,128)} %copy.29.table), custom_call_target="tpu_custom_call" | custom-call | flops 1000000000 | bytes 5505024 | tf_op jit(solution)/shard_map/pallas_call | solution.py:457
  23.1 3.3 pad_maximum_fusion.x_ref.x
  26.4 3.4 pad_maximum_fusion.1.g
  29.8 12.5 %shard_map.246 = (bf16[2,1024,768]{2,1,0:T(8,128)(2,1)}, bf16[2,1024,768]{2,1,0:T(8,128)(2,1)}, bf16[2,1024,768]{2,1,0:T(8,128)(2,1)}, bf16[2,1024,768]{2,1,0:T(8,128)(2,1)}) custom-call(s32[8]{0:T(128)} %pad_add_fusion.meta, bf16[2,1024,768]{2,1,0:T(8,128)(2,1)} %pad_maximum_fusion.x_ref.x, f32[1,768]{1,0:T(1,128)} %broadcast_in_dim.6.gain, ...), custom_call_target="tpu_custom_call" | custom-call | flops 7247757312 | bytes 15728640 | tf_op jit(solution)/shard_map/pallas_call | solution.py:468
  42.3 33.8 %shard_map.248 = (bf16[12,2,512,512]{3,2,1,0:T(8,128)(2,1)}, bf16[12,4,256,256]{3,2,1,0:T(8,128)(2,1)}, bf16[2,1024,768]{2,1,0:T(8,128)(2,1)}) custom-call(s32[8]{0:T(128)} %pad_add_fusion.meta, bf16[2,1024,768]{2,1,0:T(8,128)(2,1)} %get-tuple-element.53.q, bf16[2,1024,768]{2,1,0:T(8,128)(2,1)} %get-tuple-element.54.k, ...), custom_call_target="tpu_custom_call" | custom-call | flops 9663676416 | bytes 18874368 | tf_op jit(solution)/shard_map/pallas_call | solution.py:481
  76.1 9.2 %shard_map.249 = (f32[2,1024,768]{2,1,0:T(8,128)}, bf16[2,1024,768]{2,1,0:T(8,128)(2,1)}) custom-call(s32[8]{0:T(128)} %pad_add_fusion.meta, bf16[2,1024,768]{2,1,0:T(8,128)(2,1)} %get-tuple-element.56.attn, bf16[2,1024,768]{2,1,0:T(8,128)(2,1)} %pad_maximum_fusion.x_ref.x, bf16[768,768]{1,0:T(8,128)(2,1)} %w_out.3, f32[1,768]{1,0:T(1,128)} %broadcast_in_dim.7.gain), custom_call_target="tpu_custom_call" | custom-call | flops 2415919104 | bytes 15728640 | tf_op jit(solution)/shard_map/pallas_call | solution.py:496
  85.3 32.9 %shard_map.250 = (bf16[2,1024,3072]{2,1,0:T(8,128)(2,1)}, bf16[2,1024,3072]{2,1,0:T(8,128)(2,1)}) custom-call(s32[8]{0:T(128)} %pad_add_fusion.meta, bf16[2,1024,768]{2,1,0:T(8,128)(2,1)} %get-tuple-element.57.normed, bf16[2,1024,768]{2,1,0:T(8,128)(2,1)} %pad_maximum_fusion.1.g, bf16[768,3072]{1,0:T(8,128)(2,1)} %w_in.3, bf16[3072,768]{1,0:T(8,128)(2,1)} %w_back.3), custom_call_target="tpu_custom_call" | custom-call | flops 19327352832 | bytes 25165824 | tf_op jit(solution)/shard_map/pallas_call | solution.py:510
  118.2 16.0 %shard_map.257 = (bf16[768,1536]{1,0:T(8,128)(2,1)}, bf16[768,1536]{1,0:T(8,128)(2,1)}) custom-call(s32[8]{0:T(128)} %pad_add_fusion.meta, bf16[2,1024,768]{2,1,0:T(8,128)(2,1)} %get-tuple-element.57.normed, bf16[2,1024,3072]{2,1,0:T(8,128)(2,1)} %get-tuple-element.60.d_inner), custom_call_target="tpu_custom_call" | custom-call | flops 9663676416 | bytes 12582912 | tf_op jit(solution)/shard_map/pallas_call | solution.py:537
  134.3 31.7 %shard_map.252 = (bf16[2,1024,768]{2,1,0:T(8,128)(2,1)}, bf16[2,1024,768]{2,1,0:T(8,128)(2,1)}, f32[8,768]{1,0:T(8,128)}, bf16[768,384]{1,0:T(8,128)(2,1)}, bf16[768,384]{1,0:T(8,128)(2,1)}) custom-call(s32[8]{0:T(128)} %pad_add_fusion.meta, bf16[2,1024,3072]{2,1,0:T(8,128)(2,1)} %get-tuple-element.60.d_inner, bf16[768,3072]{1,0:T(8,128)(2,1)} %w_in.3, ...), custom_call_target="tpu_custom_call" | custom-call | flops 14495514624 | bytes 12582912 | tf_op jit(solution)/shard_map/pallas_call | solution.py:551
  166.0 23.1 %shard_map.253 = (bf16[2,1024,256]{2,1,0:T(8,128)(2,1)}, bf16[2,1024,256]{2,1,0:T(8,128)(2,1)}, bf16[2,1024,256]{2,1,0:T(8,128)(2,1)}, f32[2,8,128]{2,1,0:T(8,12...) custom-call(s32[8]{0:T(128)} %pad_add_fusion.meta, bf16[2,1024,768]{2,1,0:T(8,128)(2,1)} %get-tuple-element.53.q, ...), custom_call_target="tpu_custom_call" | custom-call | flops 8858370048 | bytes 6291456 | tf_op jit(solution)/shard_map/pallas_call | solution.py:591
  189.2 23.3 %shard_map.254 = (bf16[2,1024,256]{2,1,0:T(8,128)(2,1)}, bf16[2,1024,256]{2,1,0:T(8,128)(2,1)}, bf16[2,1024,256]{2,1,0:T(8,128)(2,1)}, f32[2,8,128]{2,1,0:T(8,12...) custom-call(s32[8]{0:T(128)} %pad_add_fusion.meta, bf16[2,1024,768]{2,1,0:T(8,128)(2,1)} %get-tuple-element.53.q, ...), custom_call_target="tpu_custom_call" | custom-call | flops 8858370048 | bytes 6291456 | tf_op jit(solution)/shard_map/pallas_call | solution.py:591
  212.5 23.1 %shard_map.255 = (bf16[2,1024,256]{2,1,0:T(8,128)(2,1)}, bf16[2,1024,256]{2,1,0:T(8,128)(2,1)}, bf16[2,1024,256]{2,1,0:T(8,128)(2,1)}, f32[2,8,128]{2,1,0:T(8,12...) custom-call(s32[8]{0:T(128)} %pad_add_fusion.meta, bf16[2,1024,768]{2,1,0:T(8,128)(2,1)} %get-tuple-element.53.q, ...), custom_call_target="tpu_custom_call" | custom-call | flops 8858370048 | bytes 6291456 | tf_op jit(solution)/shard_map/pallas_call | solution.py:591
  243.5 15.4 %shard_map.256 = (bf16[2,1024,768]{2,1,0:T(8,128)(2,1)}, f32[8,768]{1,0:T(8,128)}) custom-call(s32[8]{0:T(128)} %pad_add_fusion.meta, bf16[2,1024,768]{2,1,0:T(8,128)(2,1)} %copy-done.24, bf16[2,1024,768]{2,1,0:T(8,128)(2,1)} %copy-done.23, bf16[2,1024,768]{2,1,0:T(8,128)(2,1)} %copy-done.22, bf16[768,768]{1,0:T(8,128)(2,1)} %wq.3, bf16[768,768]{1,0:T(8,128)(2,1)} %wk.3, ...), custom_call_target="tpu_custom_call" | custom-call | flops 7247757312 | bytes 22020096 | tf_op jit(solution)/shard_map/pallas_call | solution.py:639
  258.8 2.8 slice_bitcast_fusion.1
  262.9 15.8 %shard_map.258 = (bf16[3072,384]{1,0:T(8,128)(2,1)}, bf16[3072,384]{1,0:T(8,128)(2,1)}) custom-call(s32[8]{0:T(128)} %pad_add_fusion.meta, bf16[2,1024,3072]{2,1,0:T(8,128)(2,1)} %get-tuple-element.58.low, bf16[2,1024,768]{2,1,0:T(8,128)(2,1)} %pad_maximum_fusion.1.g), custom_call_target="tpu_custom_call" | custom-call | flops 9663676416 | bytes 12582912 | tf_op jit(solution)/shard_map/pallas_call | solution.py:526
  278.7 16.0 %shard_map.251 = bf16[2,1024,768]{2,1,0:T(8,128)(2,1)} custom-call(s32[8]{0:T(128)} %pad_add_fusion.meta, bf16[2,1024,3072]{2,1,0:T(8,128)(2,1)} %get-tuple-element.58.low, bf16[3072,768]{1,0:T(8,128)(2,1)} %w_back.3, f32[2,1024,768]{2,1,0:T(8,128)} %get-tuple-element.59.hidden), custom_call_target="tpu_custom_call" | custom-call | flops 9663676416 | bytes 12582912 | tf_op jit(solution)/shard_map/pallas_call | solution.py:624
  298.3 42.0 %all-reduce = (f32[768]{0:T(1024)}, f32[32,12]{0,1:T(8,128)}, f32[768]{0:T(1024)}) all-reduce(f32[768]{0:T(1024)S(1)} %reduce_sum.18, f32[32,12]{0,1:T(8,128)S(1)} %bitcast.90, f32[768]{0:T(1024)S(1)} %reduce_sum.19), channel_id=1, replica_groups=mesh['rows'=16,'seq'=2] {'rows','seq'}, use_global_device_ids=true, to_apply=%region_1.2 | all-reduce | flops 1920 | bytes 15360 | tf_op jit(solution)/shard_map/psum | solution.py:651
  349.6 6.3 %collective-permute-done.20 = bf16[2,2,2,1,48,384]{5,4,3,2,1,0:T(8,128)(2,1)S(1)} collective-permute-done((bf16[2,2,2,1,48,384]{5,4,3,2,1,0:T(8,128)(2,1)S(1)}, bf16[2,2,2,1,48,384]{5,4,3,2,1,0:T(8,128)(2,1)S(1)}, u32[]{:S(2)}, u32[]{:S(2)}) %collective-permute-start.20) | collective-permute-done | bytes 294944 | tf_op jit(solution)/shard_map/ppermute | solution.py:357
  358.6 3.4 collective-permute-done.5
  363.9 6.9 %collective-permute-done.15 = bf16[2,2,2,1,48,384]{5,4,3,2,1,0:T(8,128)(2,1)S(1)} collective-permute-done((bf16[2,2,2,1,48,384]{5,4,3,2,1,0:T(8,128)(2,1)S(1)}, bf16[2,2,2,1,48,384]{5,4,3,2,1,0:T(8,128)(2,1)S(1)}, u32[]{:S(2)}, u32[]{:S(2)}) %collective-permute-start.15) | collective-permute-done | bytes 294944 | tf_op jit(solution)/shard_map/ppermute | solution.py:357
  373.2 4.4 collective-permute-done.21
  379.4 3.9 collective-permute-done.6
  384.3 4.1 collective-permute-done.11
  390.1 3.5 collective-permute-done.16
  408.3 3.0 collective-permute-done.17
  451.4 4.7 collective-permute-done.25
  457.7 16.4 %collective-permute-done.35 = bf16[2,2,1,1,192,128]{5,4,3,2,1,0:T(8,128)(2,1)S(1)} collective-permute-done((bf16[2,2,1,1,192,128]{5,4,3,2,1,0:T(8,128)(2,1)S(1)}, bf16[2,2,1,1,192,128]{5,4,3,2,1,0:T(8,128)(2,1)S(1)}, u32[]{:S(2)}, u32[]{:S(2)}) %collective-permute-start.35) | collective-permute-done | bytes 196640 | tf_op jit(solution)/shard_map/ppermute | solution.py:357
  475.7 4.4 collective-permute-done.36
  483.4 3.7 collective-permute-done.37
  490.8 2.9 collective-permute-done.27
  501.5 3.8 collective-permute-done.40
  506.8 4.6 collective-permute-done.41
  (265 shorter events, 116.4 us)
Async XLA Ops:
  5.0 18.1 %collective-permute-start = (bf16[1024,768]{1,0:T(8,128)(2,1)}, bf16[1024,768]{1,0:T(8,128)(2,1)}, u32[]{:S(2)}, u32[]{:S(2)}) collective-permute-start(bf16[1024,768]{1,0:T(8,128)(2,1)} %pad_maximum_fusion.2), channel_id=1, source_target_pairs={{0,1},{1,0},{2,3},{3,2},{4,5},{5,4},{6,7},{7,6},{8,9},{9,8},{10,11... | collective-permute-start | bytes 4718600 | tf_op jit(solution)/shard_map/ppermute | solution.py:357
  6.8 19.7 %collective-permute-start.1 = (bf16[1024,768]{1,0:T(8,128)(2,1)}, bf16[1024,768]{1,0:T(8,128)(2,1)}, u32[]{:S(2)}, u32[]{:S(2)}) collective-permute-start(bf16[1024,768]{1,0:T(8,128)(2,1)} %pad_maximum_fusion.3), channel_id=1, source_target_pairs={{0,1},{1,0},{2,3},{3,2},{4,5},{5,4},{6,7},{7,6},{8,9},{9,8},{10,11... | collective-permute-start | bytes 4718600 | tf_op jit(solution)/shard_map/ppermute | solution.py:357
  294.7 143.8 %collective-permute-start.33 = (bf16[3072,384]{1,0:T(8,128)(2,1)}, bf16[3072,384]{1,0:T(8,128)(2,1)}, u32[]{:S(2)}, u32[]{:S(2)}) collective-permute-start(bf16[3072,384]{1,0:T(8,128)(2,1)} %get-tuple-element.92), channel_id=1, source_target_pairs={{0,1},{1,0},{2,3},{3,2},{4,5},{5,4},{6,7},{7,6},{8,9},{9,8},{10,11... | collective-permute-start | bytes 7077896 | tf_op jit(solution)/shard_map/ppermute | solution.py:357
  295.1 147.7 %collective-permute-start.24 = (bf16[768,1536]{1,0:T(8,128)(2,1)}, bf16[768,1536]{1,0:T(8,128)(2,1)}, u32[]{:S(2)}, u32[]{:S(2)}) collective-permute-start(bf16[768,1536]{1,0:T(8,128)(2,1)} %get-tuple-element.90), channel_id=1, source_target_pairs={{0,1},{1,0},{2,3},{3,2},{4,5},{5,4},{6,7},{7,6},{8,9},{9,8},{10,11... | collective-permute-start | bytes 7077896 | tf_op jit(solution)/shard_map/ppermute | solution.py:357
  295.2 46.8 %collective-permute-start.19 = (bf16[768,384]{1,0:T(8,128)(2,1)}, bf16[768,384]{1,0:T(8,128)(2,1)}, u32[]{:S(2)}, u32[]{:S(2)}) collective-permute-start(bf16[768,384]{1,0:T(8,128)(2,1)} %get-tuple-element.84), channel_id=1, source_target_pairs={{0,1},{1,0},{2,3},{3,2},{4,5},{5,4},{6,7},{7,6},{8,9},{9,8},{10,11... | collective-permute-start | bytes 1769480 | tf_op jit(solution)/shard_map/ppermute | solution.py:357
  295.6 48.7 %collective-permute-start.4 = (bf16[768,384]{1,0:T(8,128)(2,1)}, bf16[768,384]{1,0:T(8,128)(2,1)}, u32[]{:S(2)}, u32[]{:S(2)}) collective-permute-start(bf16[768,384]{1,0:T(8,128)(2,1)} %get-tuple-element.78), channel_id=1, source_target_pairs={{0,1},{1,0},{2,3},{3,2},{4,5},{5,4},{6,7},{7,6},{8,9},{9,8},{10,11... | collective-permute-start | bytes 1769480 | tf_op jit(solution)/shard_map/ppermute | solution.py:357
  295.7 50.0 %collective-permute-start.9 = (bf16[768,384]{1,0:T(8,128)(2,1)}, bf16[768,384]{1,0:T(8,128)(2,1)}, u32[]{:S(2)}, u32[]{:S(2)}) collective-permute-start(bf16[768,384]{1,0:T(8,128)(2,1)} %get-tuple-element.80), channel_id=1, source_target_pairs={{0,1},{1,0},{2,3},{3,2},{4,5},{5,4},{6,7},{7,6},{8,9},{9,8},{10,11... | collective-permute-start | bytes 1769480 | tf_op jit(solution)/shard_map/ppermute | solution.py:357
  342.0 7.2 %collective-permute-start.14 = (bf16[768,384]{1,0:T(8,128)(2,1)}, bf16[768,384]{1,0:T(8,128)(2,1)S(1)}, u32[]{:S(2)}, u32[]{:S(2)}) collective-permute-start(bf16[768,384]{1,0:T(8,128)(2,1)} %get-tuple-element.82), channel_id=1, source_target_pairs={{0,1},{1,0},{2,3},{3,2},{4,5},{5,4},{6,7},{7,6},{8,9},{9,8},{10,11... | collective-permute-start | bytes 1769480 | tf_op jit(solution)/shard_map/ppermute | solution.py:357
  344.3 87.4 %collective-permute-start.3 = (bf16[1024,768]{1,0:T(8,128)(2,1)S(1)}, bf16[1024,768]{1,0:T(8,128)(2,1)S(1)}, u32[]{:S(2)}, u32[]{:S(2)}) collective-permute-start(bf16[1024,768]{1,0:T(8,128)(2,1)S(1)} %copy-done.6), channel_id=1, source_target_pairs={{0,1},{1,0},{2,3},{3,2},{4,5},{5,4},{6,7},{7,6},{8,9},{9,8},{10,11... | collective-permute-start | bytes 4718600 | tf_op jit(solution)/shard_map/ppermute | solution.py:357
  345.7 10.2 %collective-permute-start.20 = (bf16[2,2,2,1,48,384]{5,4,3,2,1,0:T(8,128)(2,1)S(1)}, bf16[2,2,2,1,48,384]{5,4,3,2,1,0:T(8,128)(2,1)S(1)}, u32[]{:S(2)}, u32[]{:S(2)}) collective-permute-start(bf16[2,2,2,1,48,384]{5,4,3,2,1,0:T(8,128)(2,1)S(1)} %constant_dynamic-slice_fusion.19), channel_id=1, source_target_pairs={{0,2},{2,0},{4,6},{6,4},{8,10},{10,8},{12,14},{14,12},{16,18},{18,... | collective-permute-start | bytes 884744 | tf_op jit(solution)/shard_map/ppermute | solution.py:357
  349.3 12.7 %collective-permute-start.5 = (bf16[2,2,2,1,48,384]{5,4,3,2,1,0:T(8,128)(2,1)S(1)}, bf16[2,2,2,1,48,384]{5,4,3,2,1,0:T(8,128)(2,1)S(1)}, u32[]{:S(2)}, u32[]{:S(2)}) collective-permute-start(bf16[2,2,2,1,48,384]{5,4,3,2,1,0:T(8,128)(2,1)S(1)} %constant_dynamic-slice_fusion.31), channel_id=1, source_target_pairs={{0,2},{2,0},{4,6},{6,4},{8,10},{10,8},{12,14},{14,12},{16,18},{18,... | collective-permute-start | bytes 884744 | tf_op jit(solution)/shard_map/ppermute | solution.py:357
  355.9 15.0 %collective-permute-start.10 = (bf16[2,2,1,2,48,384]{5,4,3,2,1,0:T(8,128)(2,1)S(1)}, bf16[2,2,1,2,48,384]{5,4,3,2,1,0:T(8,128)(2,1)S(1)}, u32[]{:S(2)}, u32[]{:S(2)}) collective-permute-start(bf16[2,2,1,2,48,384]{5,4,3,2,1,0:T(8,128)(2,1)S(1)} %constant_dynamic-slice_fusion.27), channel_id=1, source_target_pairs={{0,4},{2,6},{4,0},{6,2},{8,12},{10,14},{12,8},{14,10},{16,20},{18,... | collective-permute-start | bytes 884744 | tf_op jit(solution)/shard_map/ppermute | solution.py:357
  362.0 8.8 %collective-permute-start.15 = (bf16[2,2,2,1,48,384]{5,4,3,2,1,0:T(8,128)(2,1)S(1)}, bf16[2,2,2,1,48,384]{5,4,3,2,1,0:T(8,128)(2,1)S(1)}, u32[]{:S(2)}, u32[]{:S(2)}) collective-permute-start(bf16[2,2,2,1,48,384]{5,4,3,2,1,0:T(8,128)(2,1)S(1)} %constant_dynamic-slice_fusion.23), channel_id=1, source_target_pairs={{0,2},{2,0},{4,6},{6,4},{8,10},{10,8},{12,14},{14,12},{16,18},{18,... | collective-permute-start | bytes 884744 | tf_op jit(solution)/shard_map/ppermute | solution.py:357
  370.8 64.8 %collective-permute-start.2 = (bf16[1024,768]{1,0:T(8,128)(2,1)S(1)}, bf16[1024,768]{1,0:T(8,128)(2,1)S(1)}, u32[]{:S(2)}, u32[]{:S(2)}) collective-permute-start(bf16[1024,768]{1,0:T(8,128)(2,1)S(1)} %slice_bitcast_fusion), channel_id=1, source_target_pairs={{0,1},{1,0},{2,3},{3,2},{4,5},{5,4},{6,7},{7,6},{8,9},{9,8},{10,11... | collective-permute-start | bytes 4718600 | tf_op jit(solution)/shard_map/ppermute | solution.py:357
  370.9 6.7 %collective-permute-start.21 = (bf16[2,2,1,1,48,384]{5,4,3,2,1,0:T(8,128)(2,1)S(1)}, bf16[2,2,1,1,48,384]{5,4,3,2,1,0:T(8,128)(2,1)S(1)}, u32[]{:S(2)}, u32[]{:S(2)}) collective-permute-start(bf16[2,2,1,1,48,384]{5,4,3,2,1,0:T(8,128)(2,1)S(1)} %constant_dynamic-slice_fusion.18), channel_id=1, source_target_pairs={{0,4},{2,6},{4,0},{6,2},{8,12},{10,14},{12,8},{14,10},{16,20},{18,... | collective-permute-start | bytes 442376 | tf_op jit(solution)/shard_map/ppermute | solution.py:357
  377.6 5.7 %collective-permute-start.6 = (bf16[2,2,1,1,48,384]{5,4,3,2,1,0:T(8,128)(2,1)S(1)}, bf16[2,2,1,1,48,384]{5,4,3,2,1,0:T(8,128)(2,1)S(1)}, u32[]{:S(2)}, u32[]{:S(2)}) collective-permute-start(bf16[2,2,1,1,48,384]{5,4,3,2,1,0:T(8,128)(2,1)S(1)} %constant_dynamic-slice_fusion.30), channel_id=1, source_target_pairs={{0,4},{2,6},{4,0},{6,2},{8,12},{10,14},{12,8},{14,10},{16,20},{18,... | collective-permute-start | bytes 442376 | tf_op jit(solution)/shard_map/ppermute | solution.py:357
  441.9 7.8 %collective-permute-start.34 = (bf16[2,2,2,1,192,128]{5,4,3,2,1,0:T(8,128)(2,1)S(1)}, bf16[2,2,2,1,192,128]{5,4,3,2,1,0:T(8,128)(2,1)S(1)}, u32[]{:S(2)}, u32[]{:S(2)}) collective-permute-start(bf16[2,2,2,1,192,128]{5,4,3,2,1,0:T(8,128)(2,1)S(1)} %constant_dynamic-slice_fusion.7), channel_id=1, source_target_pairs={{0,2},{2,0},{4,6},{6,4},{8,10},{10,8},{12,14},{14,12},{16,18},{18,... | collective-permute-start | bytes 1179656 | tf_op jit(solution)/shard_map/ppermute | solution.py:357
  446.0 10.0 %collective-permute-start.25 = (bf16[2,2,2,1,48,768]{5,4,3,2,1,0:T(8,128)(2,1)S(1)}, bf16[2,2,2,1,48,768]{5,4,3,2,1,0:T(8,128)(2,1)S(1)}, u32[]{:S(2)}, u32[]{:S(2)}) collective-permute-start(bf16[2,2,2,1,48,768]{5,4,3,2,1,0:T(8,128)(2,1)S(1)} %constant_dynamic-slice_fusion.15), channel_id=1, source_target_pairs={{0,2},{2,0},{4,6},{6,4},{8,10},{10,8},{12,14},{14,12},{16,18},{18,... | collective-permute-start | bytes 1769480 | tf_op jit(solution)/shard_map/ppermute | solution.py:357
  447.0 40.1 %collective-permute-start.38 = (bf16[2,2,1,2,192,256]{5,4,3,2,1,0:T(8,128)(2,1)S(1)}, bf16[2,2,1,2,192,256]{5,4,3,2,1,0:T(8,128)(2,1)S(1)}, u32[]{:S(2)}, u32[]{:S(2)}) collective-permute-start(bf16[2,2,1,2,192,256]{5,4,3,2,1,0:T(8,128)(2,1)S(1)} %constant_dynamic-slice_fusion.3), channel_id=1, source_target_pairs={{0,4},{2,6},{4,0},{6,2},{8,12},{10,14},{12,8},{14,10},{16,20},{18,... | collective-permute-start | bytes 2359304 | tf_op jit(solution)/shard_map/ppermute | solution.py:357
  448.3 27.3 %collective-permute-start.29 = (bf16[2,2,1,2,48,768]{5,4,3,2,1,0:T(8,128)(2,1)S(1)}, bf16[2,2,1,2,48,768]{5,4,3,2,1,0:T(8,128)(2,1)S(1)}, u32[]{:S(2)}, u32[]{:S(2)}) collective-permute-start(bf16[2,2,1,2,48,768]{5,4,3,2,1,0:T(8,128)(2,1)S(1)} %constant_dynamic-slice_fusion.11), channel_id=1, source_target_pairs={{0,4},{2,6},{4,0},{6,2},{8,12},{10,14},{12,8},{14,10},{16,20},{18,... | collective-permute-start | bytes 1769480 | tf_op jit(solution)/shard_map/ppermute | solution.py:357
  449.8 24.3 %collective-permute-start.35 = (bf16[2,2,1,1,192,128]{5,4,3,2,1,0:T(8,128)(2,1)S(1)}, bf16[2,2,1,1,192,128]{5,4,3,2,1,0:T(8,128)(2,1)S(1)}, u32[]{:S(2)}, u32[]{:S(2)}) collective-permute-start(bf16[2,2,1,1,192,128]{5,4,3,2,1,0:T(8,128)(2,1)S(1)} %constant_dynamic-slice_fusion.6), channel_id=1, source_target_pairs={{0,4},{2,6},{4,0},{6,2},{8,12},{10,14},{12,8},{14,10},{16,20},{18,... | collective-permute-start | bytes 589832 | tf_op jit(solution)/shard_map/ppermute | solution.py:357
  456.2 32.2 %collective-permute-start.26 = (bf16[2,2,1,1,48,768]{5,4,3,2,1,0:T(8,128)(2,1)S(1)}, bf16[2,2,1,1,48,768]{5,4,3,2,1,0:T(8,128)(2,1)S(1)}, u32[]{:S(2)}, u32[]{:S(2)}) collective-permute-start(bf16[2,2,1,1,48,768]{5,4,3,2,1,0:T(8,128)(2,1)S(1)} %constant_dynamic-slice_fusion.14), channel_id=1, source_target_pairs={{0,4},{2,6},{4,0},{6,2},{8,12},{10,14},{12,8},{14,10},{16,20},{18,... | collective-permute-start | bytes 884744 | tf_op jit(solution)/shard_map/ppermute | solution.py:357
  474.3 5.9 %collective-permute-start.36 = (bf16[2,1,1,1,192,128]{5,4,3,2,1,0:T(8,128)(2,1)S(1)}, bf16[2,1,1,1,192,128]{5,4,3,2,1,0:T(8,128)(2,1)S(1)}, u32[]{:S(2)}, u32[]{:S(2)}) collective-permute-start(bf16[2,1,1,1,192,128]{5,4,3,2,1,0:T(8,128)(2,1)S(1)} %constant_dynamic-slice_fusion.5), channel_id=1, source_target_pairs={{0,8},{2,10},{4,12},{6,14},{8,0},{10,2},{12,4},{14,6},{16,24},{18,... | collective-permute-start | bytes 294920 | tf_op jit(solution)/shard_map/ppermute | solution.py:357
  480.2 6.9 %collective-permute-start.37 = (bf16[1,1,1,1,192,128]{5,4,3,2,1,0:T(8,128)(2,1)S(1)}, bf16[1,1,1,1,192,128]{5,4,3,2,1,0:T(8,128)(2,1)S(1)}, u32[]{:S(2)}, u32[]{:S(2)}) collective-permute-start(bf16[1,1,1,1,192,128]{5,4,3,2,1,0:T(8,128)(2,1)S(1)} %constant_dynamic-slice_fusion.4), channel_id=1, source_target_pairs={{0,16},{2,18},{4,20},{6,22},{8,24},{10,26},{12,28},{14,30},{16,0},... | collective-permute-start | bytes 147464 | tf_op jit(solution)/shard_map/ppermute | solution.py:357
  481.9 6.8 %collective-permute-start.30 = (bf16[2,2,1,1,48,768]{5,4,3,2,1,0:T(8,128)(2,1)S(1)}, bf16[2,2,1,1,48,768]{5,4,3,2,1,0:T(8,128)(2,1)S(1)}, u32[]{:S(2)}, u32[]{:S(2)}) collective-permute-start(bf16[2,2,1,1,48,768]{5,4,3,2,1,0:T(8,128)(2,1)S(1)} %constant_dynamic-slice_fusion.10), channel_id=1, source_target_pairs={{0,2},{2,0},{4,6},{6,4},{8,10},{10,8},{12,14},{14,12},{16,18},{18,... | collective-permute-start | bytes 884744 | tf_op jit(solution)/shard_map/ppermute | solution.py:357
  487.4 12.0 %collective-permute-start.39 = (bf16[2,2,1,1,192,256]{5,4,3,2,1,0:T(8,128)(2,1)S(1)}, bf16[2,2,1,1,192,256]{5,4,3,2,1,0:T(8,128)(2,1)S(1)}, u32[]{:S(2)}, u32[]{:S(2)}) collective-permute-start(bf16[2,2,1,1,192,256]{5,4,3,2,1,0:T(8,128)(2,1)S(1)} %constant_dynamic-slice_fusion.2), channel_id=1, source_target_pairs={{0,2},{2,0},{4,6},{6,4},{8,10},{10,8},{12,14},{14,12},{16,18},{18,... | collective-permute-start | bytes 1179656 | tf_op jit(solution)/shard_map/ppermute | solution.py:357
  488.5 5.2 %collective-permute-start.27 = (bf16[2,1,1,1,48,768]{5,4,3,2,1,0:T(8,128)(2,1)S(1)}, bf16[2,1,1,1,48,768]{5,4,3,2,1,0:T(8,128)(2,1)S(1)}, u32[]{:S(2)}, u32[]{:S(2)}) collective-permute-start(bf16[2,1,1,1,48,768]{5,4,3,2,1,0:T(8,128)(2,1)S(1)} %constant_dynamic-slice_fusion.13), channel_id=1, source_target_pairs={{0,8},{2,10},{4,12},{6,14},{8,0},{10,2},{12,4},{14,6},{16,24},{18,... | collective-permute-start | bytes 442376 | tf_op jit(solution)/shard_map/ppermute | solution.py:357
  488.8 6.5 %collective-permute-start.31 = (bf16[2,1,1,1,48,768]{5,4,3,2,1,0:T(8,128)(2,1)S(1)}, bf16[2,1,1,1,48,768]{5,4,3,2,1,0:T(8,128)(2,1)S(1)}, u32[]{:S(2)}, u32[]{:S(2)}) collective-permute-start(bf16[2,1,1,1,48,768]{5,4,3,2,1,0:T(8,128)(2,1)S(1)} %constant_dynamic-slice_fusion.9), channel_id=1, source_target_pairs={{0,8},{2,10},{4,12},{6,14},{8,0},{10,2},{12,4},{14,6},{16,24},{18,... | collective-permute-start | bytes 442376 | tf_op jit(solution)/shard_map/ppermute | solution.py:357
  493.8 5.5 %collective-permute-start.28 = (bf16[1,1,1,1,48,768]{5,4,3,2,1,0:T(8,128)(2,1)S(1)}, bf16[1,1,1,1,48,768]{5,4,3,2,1,0:T(8,128)(2,1)S(1)}, u32[]{:S(2)}, u32[]{:S(2)}) collective-permute-start(bf16[1,1,1,1,48,768]{5,4,3,2,1,0:T(8,128)(2,1)S(1)} %constant_dynamic-slice_fusion.12), channel_id=1, source_target_pairs={{0,16},{2,18},{4,20},{6,22},{8,24},{10,26},{12,28},{14,30},{16,0},... | collective-permute-start | bytes 221192 | tf_op jit(solution)/shard_map/ppermute | solution.py:357
  495.4 6.1 %collective-permute-start.32 = (bf16[1,1,1,1,48,768]{5,4,3,2,1,0:T(8,128)(2,1)S(1)}, bf16[1,1,1,1,48,768]{5,4,3,2,1,0:T(8,128)(2,1)S(1)}, u32[]{:S(2)}, u32[]{:S(2)}) collective-permute-start(bf16[1,1,1,1,48,768]{5,4,3,2,1,0:T(8,128)(2,1)S(1)} %constant_dynamic-slice_fusion.8), channel_id=1, source_target_pairs={{0,16},{2,18},{4,20},{6,22},{8,24},{10,26},{12,28},{14,30},{16,0},... | collective-permute-start | bytes 221192 | tf_op jit(solution)/shard_map/ppermute | solution.py:357
  499.5 5.7 %collective-permute-start.40 = (bf16[2,1,1,1,192,256]{5,4,3,2,1,0:T(8,128)(2,1)S(1)}, bf16[2,1,1,1,192,256]{5,4,3,2,1,0:T(8,128)(2,1)S(1)}, u32[]{:S(2)}, u32[]{:S(2)}) collective-permute-start(bf16[2,1,1,1,192,256]{5,4,3,2,1,0:T(8,128)(2,1)S(1)} %constant_dynamic-slice_fusion.1), channel_id=1, source_target_pairs={{0,8},{2,10},{4,12},{6,14},{8,0},{10,2},{12,4},{14,6},{16,24},{18,... | collective-permute-start | bytes 589832 | tf_op jit(solution)/shard_map/ppermute | solution.py:357
  505.3 6.1 %collective-permute-start.41 = (bf16[1,1,1,1,192,256]{5,4,3,2,1,0:T(8,128)(2,1)S(1)}, bf16[1,1,1,1,192,256]{5,4,3,2,1,0:T(8,128)(2,1)S(1)}, u32[]{:S(2)}, u32[]{:S(2)}) collective-permute-start(bf16[1,1,1,1,192,256]{5,4,3,2,1,0:T(8,128)(2,1)S(1)} %constant_dynamic-slice_fusion), channel_id=1, source_target_pairs={{0,16},{2,18},{4,20},{6,22},{8,24},{10,26},{12,28},{14,30},{16,0},... | collective-permute-start | bytes 294920 | tf_op jit(solution)/shard_map/ppermute | solution.py:357
  (42 other events, 256.1 us)
